TPU v7x, 32 devices: a whole 2x2x4 slice. The times are simulated.
32 devices in a mesh: src: 8 (over y, x, core), gz: 4 (over z).
Axes of the slice: x: 2, y: 2, z: 4, core: 2. Of those that a mesh axis runs over, the one named last changes fastest.
Arguments:
- travel_times: float32 [8, 16, 128, 256], P('src', 'gz'), may hold values from -6 to 6
- upwind_codes: int32 [8, 16, 128, 256], P('src', 'gz'), may hold values from 0 to 511
- adjoint_state: float32 [8, 16, 128, 256], P('src', 'gz'), may hold values from -6 to 6
- surface_residual: float32 [8, 128, 256], P('src'), may hold values from -6 to 6
- source_cell: int32 [8], P('src'), may hold values from 0 to 524287
- slowness: float32 [16, 128, 256], P('gz'), may hold values from 0.2 to 1
Outputs:
- adjoint_next: float32 [8, 16, 128, 256], P('src', 'gz')
- coarse_kernel: float32 [8, 64, 128], P('gz')
Inputs may be any that keep to these rules, and one draw needn't show every extreme that they name: `upwind_codes`: each code holds for x, y and z (bits 0 to 2, 3 to 5, 6 to 8) a low-side bit, a high-side bit and a double-weight bit; codes may name neighbours outside the grid.
All inputs are finite; a program needn't handle non-finite values.
Results may differ from a plain program's by a relative error of at most 0.0003.
Values sent between devices are 32-bit elements; how exact they have to be, the bound alone decides.
A program may use at most 128 MiB of HBM per device.

v0:
```python
import jax
import jax.numpy as jnp
from jax import lax
from jax.sharding import PartitionSpec as P


def extended_2(x, sides, width):
    for axis, dim in sides:
        devices, length = (lax.axis_size(axis), x.shape[dim])
        up = [(i, (i + 1) % devices) for i in range(devices - 1)]
        down = [(j, i) for i, j in up]
        last = lax.slice_in_dim(x, length - width, length, axis=dim)
        leading = lax.slice_in_dim(x, 0, width, axis=dim)
        before = lax.ppermute(last, axis, up)
        after = lax.ppermute(leading, axis, down)
        x = jnp.concatenate([before, x, after], axis=dim)
    return x


def axis_pair(centre, low_side, high_side, code_field, low_ok, high_ok):
    used_low = (code_field % 2).astype(jnp.float32)
    used_high = (code_field // 2 % 2).astype(jnp.float32)
    factor = 1.0 + (code_field // 4 % 2).astype(jnp.float32)
    weight_low = factor * used_low * low_ok * jnp.abs(centre - low_side)
    weight_high = factor * used_high * high_ok * jnp.abs(centre - high_side)
    return (weight_low, weight_high)


def local_weights(times_ext, codes_ext, centre_first, total_depth):
    centre = times_ext[:, 1:-1]
    code_layer = codes_ext[:, 1:-1]
    layer_count = centre.shape[1]
    row_count = centre.shape[2]
    col_count = centre.shape[3]
    z_position = centre_first + jnp.arange(layer_count)
    low_ok_z = (z_position >= 1).astype(jnp.float32)[None, :, None, None]
    high_ok_z = (z_position <= total_depth - 2).astype(jnp.float32)[None, :, None, None]
    y_index = jnp.arange(row_count)[None, None, :, None]
    x_index = jnp.arange(col_count)[None, None, None, :]
    padded_y = jnp.pad(centre, ((0, 0), (0, 0), (1, 1), (0, 0)))
    padded_x = jnp.pad(centre, ((0, 0), (0, 0), (0, 0), (1, 1)))
    low_z, high_z = axis_pair(
        centre, times_ext[:, :-2], times_ext[:, 2:], code_layer // 64 % 8, low_ok_z, high_ok_z
    )
    low_y, high_y = axis_pair(
        centre,
        padded_y[:, :, :-2],
        padded_y[:, :, 2:],
        code_layer // 8 % 8,
        (y_index >= 1).astype(jnp.float32),
        (y_index <= row_count - 2).astype(jnp.float32),
    )
    low_x, high_x = axis_pair(
        centre,
        padded_x[:, :, :, :-2],
        padded_x[:, :, :, 2:],
        code_layer % 8,
        (x_index >= 1).astype(jnp.float32),
        (x_index <= col_count - 2).astype(jnp.float32),
    )
    return (low_z, high_z, low_y, high_y, low_x, high_x)


def finish_sweep(middle, incoming, weights, out_first, total_depth, surface_residual, source_cell):
    low_z, high_z, low_y, high_y, low_x, high_x = weights
    incoming = incoming + jnp.pad(high_y * middle, ((0, 0), (0, 0), (1, 0), (0, 0)))[:, :, :-1]
    incoming = incoming + jnp.pad(low_y * middle, ((0, 0), (0, 0), (0, 1), (0, 0)))[:, :, 1:]
    incoming = incoming + jnp.pad(high_x * middle, ((0, 0), (0, 0), (0, 0), (1, 0)))[:, :, :, :-1]
    incoming = incoming + jnp.pad(low_x * middle, ((0, 0), (0, 0), (0, 0), (0, 1)))[:, :, :, 1:]
    diagonal = 1.0 + low_z + high_z + low_y + high_y + low_x + high_x
    layer_count = middle.shape[1]
    row_count = middle.shape[2]
    col_count = middle.shape[3]
    z_position = (out_first + jnp.arange(layer_count))[None, :, None, None]
    y_index = jnp.arange(row_count)[None, None, :, None]
    x_index = jnp.arange(col_count)[None, None, None, :]
    flat_index = (z_position * row_count + y_index) * col_count + x_index
    inside = (z_position >= 0) & (z_position < total_depth)
    keep_mask = inside & (flat_index != source_cell[:, None, None, None])
    forcing = jnp.where(z_position == 0, surface_residual[:, None, :, :], jnp.float32(0.0))
    return jnp.where(keep_mask, (forcing + incoming) / diagonal, jnp.float32(0.0))


def relax_once(adjoint, weights, out_first, total_depth, surface_residual, source_cell):
    low_z, high_z = (weights[0], weights[1])
    incoming = (high_z * adjoint)[:, :-2] + (low_z * adjoint)[:, 2:]
    inner = tuple((piece[:, 1:-1] for piece in weights))
    return finish_sweep(
        adjoint[:, 1:-1], incoming, inner, out_first, total_depth, surface_residual, source_cell
    )


def shards(travel_times, upwind_codes, adjoint_state, surface_residual, source_cell, slowness):
    depth_local = travel_times.shape[1]
    total_depth = depth_local * lax.axis_size("gz")
    slab_start = lax.axis_index("gz") * depth_local
    stacked = jnp.stack([travel_times, upwind_codes.astype(jnp.float32)])
    extended = extended_2(stacked, (("gz", 2),), 2)
    weights = local_weights(extended[0], extended[1].astype(jnp.int32), slab_start - 1, total_depth)
    adjoint = adjoint_state
    for sweep_index in range(2):
        state_ext = extended_2(adjoint, (("gz", 1),), 1)
        adjoint = relax_once(
            state_ext, weights, slab_start, total_depth, surface_residual, source_cell
        )
    product = adjoint * slowness[None]
    source_count = product.shape[0]
    row_count = product.shape[2]
    col_count = product.shape[3]
    coarse = product.reshape(
        source_count, depth_local // 2, 2, row_count // 2, 2, col_count // 2, 2
    ).mean(axis=(2, 4, 6))
    coarse_kernel = lax.psum(jnp.sum(coarse, axis=0), "src")
    return (adjoint, coarse_kernel)


def solution(mesh):
    in_specs = (
        P("src", "gz", None, None),
        P("src", "gz", None, None),
        P("src", "gz", None, None),
        P("src", None, None),
        P("src"),
        P("gz", None, None),
    )
    out_specs = (P("src", "gz", None, None), P("gz", None, None))
    return jax.shard_map(shards, mesh=mesh, in_specs=in_specs, out_specs=out_specs, check_vma=False)
```

profile of v0, /device:TPU:0, one launch (start us, length us, event | category | flops | bytes accessed | tf_op | source)
XLA Modules:
  0.0 168.9 jit_solution(1630537265260104692)
XLA Ops:
  7.2 1.7 %fusion.92 = (f32[1,1,128,256]{3,2,1,0:T(8,128)S(1)}, f32[1,1,128,256]{3,2,1,0:T(8,128)}) fusion(f32[1,4,128,256]{3,2,1,0:T(8,128)} %param.8), kind=kLoop, calls=%fused_computation.206 | loop fusion | bytes 524288 | tf_op jit(solution)/shard_map/slice | solution.py:13
  8.9 1.3 collective-permute-start.3
  10.2 5.6 %collective-permute-start.2 = (f32[1,1,128,256]{3,2,1,0:T(8,128)}, f32[1,1,128,256]{3,2,1,0:T(8,128)S(1)}, u32[]{:S(2)}, u32[]{:S(2)}) collective-permute-start(f32[1,1,128,256]{3,2,1,0:T(8,128)} %get-tuple-element.49), channel_id=1, source_target_pairs={{0,1},{1,2},{2,3},{4,5},{5,6},{6,7},{8,9},{9,10},{10,11},{12,13},{... | collective-permute-start | bytes 393224 | tf_op jit(solution)/shard_map/ppermute | solution.py:14
  15.8 1.1 convert_bitcast_fusion
  16.9 1.1 fusion.59
  18.0 3.9 %collective-permute-start = (f32[2,1,2,128,256]{4,3,2,1,0:T(8,128)S(1)}, f32[2,1,2,128,256]{4,3,2,1,0:T(8,128)S(1)}, u32[]{:S(2)}, u32[]{:S(2)}) collective-permute-start(f32[2,1,2,128,256]{4,3,2,1,0:T(8,128)S(1)} %get-tuple-element.36), channel_id=1, source_target_pairs={{0,1},{1,2},{2,3},{4,5},{5,6},{6,7},{8,9},{9,10},{10,11},{12,13},{... | collective-permute-start | bytes 1572872 | tf_op jit(solution)/shard_map/ppermute | solution.py:14
  21.9 1.3 collective-permute-start.1
  23.2 0.5 fusion.75
  23.8 0.7 add_multiply_fusion
  25.2 7.3 %collective-permute-done = f32[2,1,2,128,256]{4,3,2,1,0:T(8,128)S(1)} collective-permute-done((f32[2,1,2,128,256]{4,3,2,1,0:T(8,128)S(1)}, f32[2,1,2,128,256]{4,3,2,1,0:T(8,128)S(1)}, u32[]{:S(2)}, u32[]{:S(2)}) %collective-permute-start) | collective-permute-done | bytes 524320 | tf_op jit(solution)/shard_map/ppermute | solution.py:14
  32.5 4.1 %collective-permute-done.1 = f32[2,1,2,128,256]{4,3,2,1,0:T(8,128)S(1)} collective-permute-done((f32[2,1,2,128,256]{4,3,2,1,0:T(8,128)S(1)}, f32[2,1,2,128,256]{4,3,2,1,0:T(8,128)S(1)}, u32[]{:S(2)}, u32[]{:S(2)}) %collective-permute-start.1) | collective-permute-done | bytes 524320 | tf_op jit(solution)/shard_map/ppermute | solution.py:15
  37.1 2.0 %fusion.15 = (f32[1,6,128,256]{3,2,1,0:T(8,128)S(1)}, pred[1,6,128,256]{3,2,1,0:T(8,128)(4,1)S(1)}) fusion(f32[1,8,128,256]{3,2,1,0:T(8,128)S(1)} %get-tuple-element.32, f32[6]{0:T(128)S(1)} %get-tuple-element.53, s32[1,8,128,256]{3,2,1,0:T(8,128)S(1)} %get-tuple-element.31), kind=kLoop, calls=%fused_computation.76 | loop fusion | flops 13369344 | bytes 3342360 | tf_op jit(solution)/shard_map/mul | solution.py:24
  39.1 1.0 broadcast_compare_fusion.2
  40.1 0.8 fusion.20
  41.0 0.8 broadcast_compare_fusion.5
  41.9 0.6 broadcast_compare_fusion.1
  42.5 3.3 %fusion.11 = (f32[1,6,128,256]{3,2,1,0:T(8,128)S(1)}, f32[1,6,128,256]{3,2,1,0:T(8,128)S(1)}, f32[1,6,128,256]{3,2,1,0:T(8,128)S(1)}) fusion(f32[1,8,128,256]{3,2,1,0:T(8,128)S(1)} %get-tuple-element.32, f32[6]{0:T(128)S(1)} %get-tuple-element.54, pred[1,6,128,256]{3,2,1,0:T(8,128)(4,1)S(1)} %get-tuple-element.16, ...), kind=kLoop, calls=%fused_computation.72 | loop fusion | flops 22413312 | bytes 5111832 | tf_op jit(solution)/shard_map/mul | solution.py:25
  45.9 1.1 broadcast_compare_fusion.6
  47.1 0.5 pad_slice_fusion.4
  47.6 0.5 copy-done
  48.1 0.5 fusion.83
  49.5 0.6 fusion.78
  50.2 3.5 %collective-permute-start.4 = (f32[1,1,128,256]{3,2,1,0:T(8,128)S(1)}, f32[1,1,128,256]{3,2,1,0:T(8,128)S(1)}, u32[]{:S(2)}, u32[]{:S(2)}) collective-permute-start(f32[1,1,128,256]{3,2,1,0:T(8,128)S(1)} %get-tuple-element.43), channel_id=1, source_target_pairs={{0,1},{1,2},{2,3},{4,5},{5,6},{6,7},{8,9},{9,10},{10,11},{12,13},{... | collective-permute-start | bytes 393224 | tf_op jit(solution)/shard_map/ppermute | solution.py:14
  53.7 1.6 collective-permute-start.5
  55.5 0.7 collective-permute-done.4
  56.2 4.5 %collective-permute-done.5 = f32[1,1,128,256]{3,2,1,0:T(8,128)S(1)} collective-permute-done((f32[1,1,128,256]{3,2,1,0:T(8,128)S(1)}, f32[1,1,128,256]{3,2,1,0:T(8,128)S(1)}, u32[]{:S(2)}, u32[]{:S(2)}) %collective-permute-start.5) | collective-permute-done | bytes 131104 | tf_op jit(solution)/shard_map/ppermute | solution.py:15
  60.8 1.3 bitcast_multiply_fusion
  62.1 34.8 %reshape.154 = f32[2,2,64,2,128,2]{5,4,3,2,1,0:T(8,128)} reshape(f32[1,4,128,256]{3,2,1,0:T(8,128)S(1)} %get-tuple-element.2) | data formatting | bytes 1048576 | tf_op jit(solution)/shard_map/reshape | solution.py:110
  96.9 12.2 %reduce_sum.8 = f32[2,64,128]{2,1,0:T(8,128)S(1)} reduce(f32[2,2,64,2,128,2]{5,4,3,2,1,0:T(8,128)} %reshape.154, f32[]{:T(128)} %constant.163.clone.1), dimensions={1,3,5}, to_apply=%region_0.1 | reduce | flops 114688 | bytes 589828 | tf_op jit(solution)/shard_map/reduce_sum | solution.py:112
  109.1 0.6 broadcast_multiply_fusion
  109.8 50.8 %all-reduce.12.cloned.1.call-done = f32[2,64,128]{2,1,0:T(8,128)} async-done(((f32[2,64,128]{2,1,0:T(8,128)}), f32[2,64,128]{2,1,0:T(8,128)}) %all-reduce.12.cloned.1.call-update) | async-done | bytes 65552 | tf_op jit(solution)/shard_map/psum | solution.py:113
  160.6 1.5 copy.12
  (26 shorter events, 2.0 us)
Async XLA Ops:
  7.2 29.5 %copy-start.1 = (f32[1,4,128,256]{3,2,1,0:T(8,128)S(1)}, f32[1,4,128,256]{3,2,1,0:T(8,128)}, u32[]{:S(2)}) copy-start(f32[1,4,128,256]{3,2,1,0:T(8,128)} %param.6) | copy-start | bytes 1572868
  7.2 153.4 %all-reduce.12.cloned.1.call-start = ((), (), s32[]{:S(2)}) async-start(), calls=%async_computation | async-start | bytes 131072 | tf_op jit(solution)/shard_map/psum | solution.py:113
  8.9 40.2 %collective-permute-start.3 = (f32[1,1,128,256]{3,2,1,0:T(8,128)S(1)}, f32[1,1,128,256]{3,2,1,0:T(8,128)S(1)}, u32[]{:S(2)}, u32[]{:S(2)}) collective-permute-start(f32[1,1,128,256]{3,2,1,0:T(8,128)S(1)} %get-tuple-element.48), channel_id=1, source_target_pairs={{1,0},{2,1},{3,2},{5,4},{6,5},{7,6},{9,8},{10,9},{11,10},{13,12},{... | collective-permute-start | bytes 393224 | tf_op jit(solution)/shard_map/ppermute | solution.py:15
  10.2 15.0 %collective-permute-start.2 = (f32[1,1,128,256]{3,2,1,0:T(8,128)}, f32[1,1,128,256]{3,2,1,0:T(8,128)S(1)}, u32[]{:S(2)}, u32[]{:S(2)}) collective-permute-start(f32[1,1,128,256]{3,2,1,0:T(8,128)} %get-tuple-element.49), channel_id=1, source_target_pairs={{0,1},{1,2},{2,3},{4,5},{5,6},{6,7},{8,9},{9,10},{10,11},{12,13},{... | collective-permute-start | bytes 393224 | tf_op jit(solution)/shard_map/ppermute | solution.py:14
  18.0 14.5 %collective-permute-start = (f32[2,1,2,128,256]{4,3,2,1,0:T(8,128)S(1)}, f32[2,1,2,128,256]{4,3,2,1,0:T(8,128)S(1)}, u32[]{:S(2)}, u32[]{:S(2)}) collective-permute-start(f32[2,1,2,128,256]{4,3,2,1,0:T(8,128)S(1)} %get-tuple-element.36), channel_id=1, source_target_pairs={{0,1},{1,2},{2,3},{4,5},{5,6},{6,7},{8,9},{9,10},{10,11},{12,13},{... | collective-permute-start | bytes 1572872 | tf_op jit(solution)/shard_map/ppermute | solution.py:14
  21.9 14.7 %collective-permute-start.1 = (f32[2,1,2,128,256]{4,3,2,1,0:T(8,128)S(1)}, f32[2,1,2,128,256]{4,3,2,1,0:T(8,128)S(1)}, u32[]{:S(2)}, u32[]{:S(2)}) collective-permute-start(f32[2,1,2,128,256]{4,3,2,1,0:T(8,128)S(1)} %get-tuple-element.37), channel_id=1, source_target_pairs={{1,0},{2,1},{3,2},{5,4},{6,5},{7,6},{9,8},{10,9},{11,10},{13,12},{... | collective-permute-start | bytes 1572872 | tf_op jit(solution)/shard_map/ppermute | solution.py:15
  47.1 1.0 copy-start
  48.6 0.9 copy-start.2
  50.2 6.0 %collective-permute-start.4 = (f32[1,1,128,256]{3,2,1,0:T(8,128)S(1)}, f32[1,1,128,256]{3,2,1,0:T(8,128)S(1)}, u32[]{:S(2)}, u32[]{:S(2)}) collective-permute-start(f32[1,1,128,256]{3,2,1,0:T(8,128)S(1)} %get-tuple-element.43), channel_id=1, source_target_pairs={{0,1},{1,2},{2,3},{4,5},{5,6},{6,7},{8,9},{9,10},{10,11},{12,13},{... | collective-permute-start | bytes 393224 | tf_op jit(solution)/shard_map/ppermute | solution.py:14
  53.7 7.1 %copy-start.3 = (f32[4,128,256]{2,1,0:T(8,128)S(1)}, f32[4,128,256]{2,1,0:T(8,128)}, u32[]{:S(2)}) copy-start(f32[4,128,256]{2,1,0:T(8,128)} %param.11) | copy-start | bytes 1572868
  53.7 7.0 %collective-permute-start.5 = (f32[1,1,128,256]{3,2,1,0:T(8,128)S(1)}, f32[1,1,128,256]{3,2,1,0:T(8,128)S(1)}, u32[]{:S(2)}, u32[]{:S(2)}) collective-permute-start(f32[1,1,128,256]{3,2,1,0:T(8,128)S(1)} %get-tuple-element.44), channel_id=1, source_target_pairs={{1,0},{2,1},{3,2},{5,4},{6,5},{7,6},{9,8},{10,9},{11,10},{13,12},{... | collective-permute-start | bytes 393224 | tf_op jit(solution)/shard_map/ppermute | solution.py:15
Sparse Core Ops, SparseCore 0:
  109.9 50.6 all-reduce.11
where the time goes:
time: 169 us
  waiting for transfers between devices  67.5 us (40%)
  local copies, waits for them, and re-layouts  39.5 us (23%)
  other arithmetic  29.8 us (18%)
  starting transfers between devices  17.2 us (10%)
  between operations  15 us (9%)
    psum x1, waiting for transfers between devices, shards(): coarse_kernel = lax.psum(jnp.sum(coarse, axis=0), 'src')  50.8 us
    reshape x1, local copies, waits for them, and re-layouts, shards(): product.reshape(source_count, depth_local // 2, 2, row_count // 2, 2, col...  34.8 us
    ppermute x3, starting transfers between devices, extended_2(): before = lax.ppermute(last, axis, up)  13 us
    reduce_sum x1, other arithmetic, shards(): coarse = product.reshape(source_count, depth_local // 2, 2, row_count //...  12.2 us
    ppermute x3, waiting for transfers between devices, extended_2(): after = lax.ppermute(leading, axis, down)  8.66 us
    ppermute x3, waiting for transfers between devices, extended_2(): before = lax.ppermute(last, axis, up)  8.04 us
    ppermute x3, starting transfers between devices, extended_2(): after = lax.ppermute(leading, axis, down)  4.18 us
  transfers between devices with their start and end apart: 7, of which 5 were waited for; matrix products, arithmetic and copies ran while one was open for 9% of the time, Pallas kernels for 0%

commit v1 on v0

v1 whole, which is shorter than its diff:
```python
import functools

import jax
import jax.numpy as jnp
from jax import lax
from jax.experimental import pallas as pl
from jax.experimental.pallas import tpu as pltpu
from jax.sharding import PartitionSpec as P

MESH = pl.DeviceIdType.MESH
CH = 32


def kernel(
    n_src, n_gz,
    t_hbm, c_hbm, a_hbm, res_hbm, cell_ref, slow_hbm,
    out_hbm, coarse_hbm,
    t, code, lam, lam1, res, slow,
    wlx, whx, wly, why, wlz, whz, diag,
    num, dface, fac, g_out, t_in, g_in,
    pool, pairs, part, rs_in, total,
    load_sem, t_send, t_recv, g_send, g_recv, rs_send, rs_recv, ag_send, ag_recv, out_sem,
):
    L, NY, NX = t.shape
    K = NY // CH
    me_s, me_z = lax.axis_index("src"), lax.axis_index("gz")
    has_lo, has_hi = me_z > 0, me_z < n_gz - 1
    layer = (0, L - 1)
    exists = (has_lo, has_hi)
    target = (me_z - 1, me_z + 1)
    f32 = jnp.float32

    barrier = pltpu.get_barrier_semaphore()
    for s in range(2):
        @pl.when(exists[s])
        def _(s=s):
            pl.semaphore_signal(barrier, 1, device_id={"gz": target[s]}, device_id_type=MESH)
    for i in range(1, n_src):
        pl.semaphore_signal(
            barrier, 1, device_id={"src": lax.rem(me_s + i, n_src)}, device_id_type=MESH
        )

    loads = {}

    def load(name, src, dst):
        copy = pltpu.make_async_copy(src, dst, load_sem.at[len(loads)])
        copy.start()
        loads[name] = copy

    order = [0, L - 1] + list(range(1, L - 1))
    for l in order[:2]:
        load(("c", l), c_hbm.at[0, l], code.at[l])
        load(("a", l), a_hbm.at[0, l], lam.at[l])
    for l in order:
        load(("t", l), t_hbm.at[0, l], t.at[l])
    for l in order[2:]:
        load(("c", l), c_hbm.at[0, l], code.at[l])
        load(("a", l), a_hbm.at[0, l], lam.at[l])
    load("res", res_hbm.at[0], res)
    for l in range(L):
        load(("s", l), slow_hbm.at[l], slow.at[l])

    def rows(k):
        return pl.ds(pl.multiple_of(k * CH, CH), CH)

    def t_copy(s, k):
        return pltpu.make_async_remote_copy(
            src_ref=t_hbm.at[0, layer[s], rows(k)], dst_ref=t_in.at[1 - s, rows(k)],
            send_sem=t_send.at[s, k], recv_sem=t_recv.at[1 - s, k],
            device_id={"gz": target[s]}, device_id_type=MESH)

    def t_arrival(s, k):
        return pltpu.make_async_remote_copy(
            src_ref=t_hbm.at[0, layer[s], rows(k)], dst_ref=t_in.at[s, rows(k)],
            send_sem=t_send.at[s, k], recv_sem=t_recv.at[s, k],
            device_id={"gz": target[s]}, device_id_type=MESH)

    def g_copy(sweep, s, k):
        return pltpu.make_async_remote_copy(
            src_ref=g_out.at[sweep, s, rows(k)], dst_ref=g_in.at[sweep, 1 - s, rows(k)],
            send_sem=g_send.at[sweep, s, k], recv_sem=g_recv.at[sweep, 1 - s, k],
            device_id={"gz": target[s]}, device_id_type=MESH)

    def g_arrival(sweep, s, k):
        return pltpu.make_async_remote_copy(
            src_ref=g_out.at[sweep, s, rows(k)], dst_ref=g_in.at[sweep, s, rows(k)],
            send_sem=g_send.at[sweep, s, k], recv_sem=g_recv.at[sweep, s, k],
            device_id={"gz": target[s]}, device_id_type=MESH)

    for s in range(2):
        @pl.when(jnp.logical_not(exists[s]))
        def _(s=s):
            t_in[s] = jnp.zeros((NY, NX), f32)
            g_in[0, s] = jnp.zeros((NY, NX), f32)
            g_in[1, s] = jnp.zeros((NY, NX), f32)

    for l in order[:2]:
        loads["c", l].wait()
        loads["a", l].wait()

    pl.semaphore_wait(
        barrier, n_src - 1 + has_lo.astype(jnp.int32) + has_hi.astype(jnp.int32)
    )

    def factors(c, shift):
        factor = jnp.where((c & (4 << shift)) != 0, f32(2.0), f32(1.0))
        low = jnp.where((c & (1 << shift)) != 0, factor, f32(0.0))
        high = jnp.where((c & (2 << shift)) != 0, factor, f32(0.0))
        return low, high

    def first_sends(k, carry):
        for s in range(2):
            @pl.when(exists[s])
            def _(s=s):
                t_copy(s, k).start()
        for s in range(2):
            f = factors(code[layer[s], rows(k)], 6)[s]
            fac[s, rows(k)] = f
            g_out[0, s, rows(k)] = f * lam[layer[s], rows(k)]
            @pl.when(exists[s])
            def _(s=s):
                g_copy(0, s, k).start()
        return carry

    lax.fori_loop(0, K, first_sends, 0)

    row_iota = lax.broadcasted_iota(jnp.int32, (CH, NX), 0)
    col = lax.broadcasted_iota(jnp.int32, (CH, NX), 1)
    cell = cell_ref[0]

    pool_row = lax.broadcasted_iota(jnp.int32, (NX, NX // 2), 0)
    pool_col = lax.broadcasted_iota(jnp.int32, (NX, NX // 2), 1)
    pool[...] = jnp.where(pool_row // 2 == pool_col, f32(0.125), f32(0.0)).astype(jnp.bfloat16)

    def before(k):
        return pl.ds(pl.multiple_of(lax.rem(k * CH + NY - 8, NY), 8), 8)

    def behind(k):
        return pl.ds(pl.multiple_of(lax.rem(k * CH + CH, NY), 8), 8)

    def from_low(prev, cur):
        return pltpu.roll(jnp.concatenate([prev, cur], axis=0), 1, 0)[8:]

    def from_high(cur, nxt):
        return pltpu.roll(jnp.concatenate([cur, nxt], axis=0), CH + 7, 0)[:CH]

    def keep_inverse(d, l, k):
        flat = (row_iota + k * CH) * NX + col
        keep = flat != cell - (me_z * L + l) * (NY * NX)
        return jnp.where(keep, 1.0 / d, f32(0.0))

    def weights(l, k):
        r = rows(k)
        row = row_iota + k * CH
        centre = t[l, r]
        c = code[l, r]
        dx = jnp.where(col == NX - 1, f32(0.0), jnp.abs(centre - pltpu.roll(centre, NX - 1, 1)))
        fl, fh = factors(c, 0)
        low, high = fl * pltpu.roll(dx, 1, 1), fh * dx
        wlx[l, r] = low
        whx[l, r] = high
        d = 1.0 + low + high
        fl, fh = factors(c, 3)
        down = jnp.abs(centre - from_low(t[l, before(k)], centre))
        up = jnp.abs(centre - from_high(centre, t[l, behind(k)]))
        low = fl * jnp.where(row == 0, f32(0.0), down)
        high = fh * jnp.where(row == NY - 1, f32(0.0), up)
        wly[l, r] = low
        why[l, r] = high
        d = d + low + high
        fl, fh = factors(c, 6)
        if l > 0:
            low = fl * jnp.abs(centre - t[l - 1, r])
            wlz[l, r] = low
            d = d + low
        if l < L - 1:
            high = fh * jnp.abs(centre - t[l + 1, r])
            whz[l, r] = high
            d = d + high
        if 0 < l < L - 1:
            d = keep_inverse(d, l, k)
        diag[l, r] = d

    top = (me_z == 0).astype(f32)

    def incoming(state, l, k):
        r, b, n = rows(k), before(k), behind(k)
        x = state[l, r]
        total_in = pltpu.roll(whx[l, r] * x, 1, 1) + pltpu.roll(wlx[l, r] * x, NX - 1, 1)
        total_in += from_low(why[l, b] * state[l, b], why[l, r] * x)
        total_in += from_high(wly[l, r] * x, wly[l, n] * state[l, n])
        if l > 0:
            total_in += whz[l - 1, r] * state[l - 1, r]
        if l < L - 1:
            total_in += wlz[l + 1, r] * state[l + 1, r]
        if l == 0:
            total_in += res[r] * top
        return total_in

    for l in order:
        loads["t", l].wait()
    for l in order[2:]:
        loads["c", l].wait()
        loads["a", l].wait()

    def all_weights(k, carry):
        for l in range(L):
            weights(l, k)
        return carry

    lax.fori_loop(0, K, all_weights, 0)
    loads["res"].wait()

    def local_sweep(state, result, k):
        for s in range(2):
            num[s, rows(k)] = incoming(state, layer[s], k)
        for l in range(1, L - 1):
            result[l, rows(k)] = incoming(state, l, k) * diag[l, rows(k)]

    def first_local(k, carry):
        local_sweep(lam, lam1, k)
        return carry

    lax.fori_loop(0, K, first_local, 0)

    def first_faces(k, carry):
        r = rows(k)
        for s in range(2):
            l = layer[s]
            @pl.when(exists[s])
            def _(s=s):
                t_arrival(s, k).wait_recv()
                g_arrival(0, s, k).wait_recv()
            d = jnp.where(exists[s], jnp.abs(t[l, r] - t_in[s, r]), f32(0.0))
            dface[s, r] = d
            f = fac[s, r]
            inverse = keep_inverse(diag[l, r] + f * d, l, k)
            diag[l, r] = inverse
            new = (num[s, r] + d * g_in[0, s, r]) * inverse
            lam1[l, r] = new
            g_out[1, s, r] = f * new
            @pl.when(exists[s])
            def _(s=s):
                g_copy(1, s, k).start()
        return carry

    lax.fori_loop(0, K, first_faces, 0)

    def second_local(k, carry):
        local_sweep(lam1, lam, k)
        return carry

    lax.fori_loop(0, K, second_local, 0)

    def out_copy(l):
        return pltpu.make_async_copy(lam.at[l], out_hbm.at[0, l], out_sem.at[l])

    for l in range(1, L - 1):
        out_copy(l).start()
    for l in range(L):
        loads["s", l].wait()

    CR = CH // 2
    CY = NY // 2
    SR = (L // 2) * CY // n_src

    def rs_copy(o):
        return pltpu.make_async_remote_copy(
            src_ref=part.at[pl.ds(pl.multiple_of(o * SR, SR), SR)], dst_ref=rs_in.at[me_s],
            send_sem=rs_send.at[o], recv_sem=rs_recv.at[me_s],
            device_id={"src": o}, device_id_type=MESH)

    def rs_arrival(j):
        return pltpu.make_async_remote_copy(
            src_ref=part.at[pl.ds(0, SR)], dst_ref=rs_in.at[j],
            send_sem=rs_send.at[j], recv_sem=rs_recv.at[j],
            device_id={"src": j}, device_id_type=MESH)

    def last_faces(k, carry):
        r = rows(k)
        for s in range(2):
            l = layer[s]
            @pl.when(exists[s])
            def _(s=s):
                g_arrival(1, s, k).wait_recv()
            lam[l, r] = (num[s, r] + dface[s, r] * g_in[1, s, r]) * diag[l, r]
        for j in range(L // 2):
            prod = lam[2 * j, r] * slow[2 * j, r] + lam[2 * j + 1, r] * slow[2 * j + 1, r]
            hi = prod.astype(jnp.bfloat16)
            lo = (prod - hi.astype(f32)).astype(jnp.bfloat16)
            pairs[j] = jnp.dot(hi, pool[...], preferred_element_type=f32) + jnp.dot(
                lo, pool[...], preferred_element_type=f32)
            first = j * CY + k * CR
            part[pl.ds(pl.multiple_of(first, CR), CR)] = (
                pairs[j, pl.ds(0, CR, stride=2)] + pairs[j, pl.ds(1, CR, stride=2)])
            for i in range(CR // SR):
                o = first // SR + i
                @pl.when(o != me_s)
                def _(o=o):
                    rs_copy(o).start()
        return carry

    lax.fori_loop(0, K, last_faces, 0)
    for s in range(2):
        out_copy(layer[s]).start()

    mine = pl.multiple_of(me_s * SR, SR)
    acc = part[pl.ds(mine, SR)]
    for i in range(1, n_src):
        j = lax.rem(me_s + i, n_src)
        rs_arrival(j).wait_recv()
        acc = acc + rs_in[j]
    total[...] = acc

    def place(o):
        return coarse_hbm.at[o * SR // CY, pl.ds(pl.multiple_of(lax.rem(o * SR, CY), SR), SR)]

    def ag_copy(i):
        o = lax.rem(me_s + i, n_src)
        return pltpu.make_async_remote_copy(
            src_ref=total, dst_ref=place(me_s),
            send_sem=ag_send.at[i], recv_sem=ag_recv.at[i],
            device_id={"src": o}, device_id_type=MESH)

    def ag_arrival(i):
        j = lax.rem(me_s + n_src - i, n_src)
        return pltpu.make_async_remote_copy(
            src_ref=total, dst_ref=place(j),
            send_sem=ag_send.at[i], recv_sem=ag_recv.at[i],
            device_id={"src": j}, device_id_type=MESH)

    for i in range(1, n_src):
        ag_copy(i).start()
    own = pltpu.make_async_copy(total, place(me_s), ag_send.at[0])
    own.start()

    def drain(k, carry):
        for s in range(2):
            @pl.when(exists[s])
            def _(s=s):
                t_copy(s, k).wait_send()
                g_copy(0, s, k).wait_send()
                g_copy(1, s, k).wait_send()
        return carry

    lax.fori_loop(0, K, drain, 0)
    for i in range(1, n_src):
        rs_copy(lax.rem(me_s + i, n_src)).wait_send()
    for l in range(L):
        out_copy(l).wait()
    own.wait()
    for i in range(1, n_src):
        ag_copy(i).wait_send()
    for i in range(1, n_src):
        ag_arrival(i).wait_recv()


def shards(n_src, n_gz, travel_times, upwind_codes, adjoint_state, surface_residual, source_cell, slowness):
    _, L, NY, NX = travel_times.shape
    K = NY // CH
    f32 = jnp.float32
    rows_total = (L // 2) * (NY // 2)
    share = rows_total // n_src
    field = pltpu.VMEM((L, NY, NX), f32)
    faces = pltpu.VMEM((2, NY, NX), f32)
    any_spec = pl.BlockSpec(memory_space=pl.ANY)
    dma = pltpu.SemaphoreType.DMA
    return pl.pallas_call(
        functools.partial(kernel, n_src, n_gz),
        out_shape=(
            jax.ShapeDtypeStruct(travel_times.shape, f32),
            jax.ShapeDtypeStruct((L // 2, NY // 2, NX // 2), f32),
        ),
        in_specs=[any_spec] * 4 + [pl.BlockSpec(memory_space=pltpu.SMEM), any_spec],
        out_specs=(any_spec, any_spec),
        scratch_shapes=[
            field, pltpu.VMEM((L, NY, NX), jnp.int32), field, field,
            pltpu.VMEM((NY, NX), f32), field,
            field, field, field, field, field, field, field,
            faces, faces, faces,
            pltpu.VMEM((2, 2, NY, NX), f32), faces, pltpu.VMEM((2, 2, NY, NX), f32),
            pltpu.VMEM((NX, NX // 2), jnp.bfloat16),
            pltpu.VMEM((L // 2, CH, NX // 2), f32),
            pltpu.VMEM((rows_total, NX // 2), f32),
            pltpu.VMEM((n_src, share, NX // 2), f32),
            pltpu.VMEM((share, NX // 2), f32),
            dma((4 * L + 1,)),
            dma((2, K)), dma((2, K)), dma((2, 2, K)), dma((2, 2, K)),
            dma((n_src,)), dma((n_src,)), dma((n_src,)), dma((n_src,)),
            dma((L,)),
        ],
        compiler_params=pltpu.CompilerParams(
            collective_id=0, has_side_effects=True, vmem_limit_bytes=48 * 1024 * 1024
        ),
    )(travel_times, upwind_codes, adjoint_state, surface_residual, source_cell, slowness)


def solution(mesh):
    in_specs = (
        P("src", "gz", None, None),
        P("src", "gz", None, None),
        P("src", "gz", None, None),
        P("src", None, None),
        P("src"),
        P("gz", None, None),
    )
    out_specs = (P("src", "gz", None, None), P("gz", None, None))
    body = functools.partial(shards, mesh.shape["src"], mesh.shape["gz"])
    return jax.shard_map(body, mesh=mesh, in_specs=in_specs, out_specs=out_specs, check_vma=False)
```

time: 169 us -> 30.6 us (0.18)
  waiting for transfers between devices: 67.5 us -> 0 us
  local copies, waits for them, and re-layouts: 39.5 us -> 6.49 us
  other arithmetic: 29.8 us -> 0 us
  Pallas kernels: 0 us -> 22.5 us
  starting transfers between devices: 17.2 us -> 0 us
  between operations: 15 us -> 1.3 us
    psum x1 -> x0, waiting for transfers between devices: 50.8 us -> none  [shards(): coarse_kernel = lax.psum(jnp.sum(coarse, axis=0), 'src')]
    reshape x1 -> x0, local copies, waits for them, and re-layouts: 34.8 us -> none  [shards(): product.reshape(source_count, depth_local // 2, 2, row_count // 2, 2, col...]
    pallas_call x0 -> x1, Pallas kernels: none -> 22.5 us  [shards(): pl.pallas_call(functools.partial(kernel, n_src, n_gz), out_shape=(jax.Sha...]
    ppermute x6 -> x0, starting transfers between devices: 17.1 us -> none  [the longest x3 13 us: extended_2(): before = lax.ppermute(last, axis, up)]
    ppermute x6 -> x0, waiting for transfers between devices: 16.7 us -> none  [the longest x3 8.66 us: extended_2(): after = lax.ppermute(leading, axis, down)]
    reduce_sum x1 -> x0, other arithmetic: 12.2 us -> none  [shards(): coarse = product.reshape(source_count, depth_local // 2, 2, row_count //...]
    mul x9 -> x0, other arithmetic: 9.62 us -> none  [the longest x1 3.34 us: axis_pair(): weight_high = factor * used_high * high_ok * jnp.abs(centre - high_side)]
    unnamed x10 -> x12, local copies, waits for them, and re-layouts: 2.37 us -> 6.49 us
  transfers between devices with their start and end apart: 7 -> 0, of which waited for: 5 -> 0; matrix products, arithmetic and copies ran while one was open for 9% -> 0% of each run, Pallas kernels for 0% -> 0%
where the time goes in v1:
time: 30.6 us; the launch traced here: 30.2 us
  Pallas kernels  22.5 us (74%)
  local copies, waits for them, and re-layouts  6.49 us (21%)
  between operations  1.3 us (4%)
    pallas_call x1, Pallas kernels, shards(): pl.pallas_call(functools.partial(kernel, n_src, n_gz), out_shape=(jax.Sha...  22.5 us
    unnamed x12, local copies, waits for them, and re-layouts  6.49 us

profile of v1, /device:TPU:0, one launch (start us, length us, event | category | flops | bytes accessed | tf_op | source)
XLA Modules:
  0.0 30.2 jit_solution(9655469629287434693)
XLA Ops:
  1.3 0.0 copy-start
  1.3 1.0 %copy-done = f32[1,4,128,256]{3,2,1,0:T(8,128)S(1)} copy-done((f32[1,4,128,256]{3,2,1,0:T(8,128)S(1)}, f32[1,4,128,256]{3,2,1,0:T(8,128)}, u32[]{:S(2)}) %copy-start) | copy-done | bytes 524312
  2.3 0.0 copy-start.1
  2.3 1.0 %copy-done.1 = s32[1,4,128,256]{3,2,1,0:T(8,128)S(1)} copy-done((s32[1,4,128,256]{3,2,1,0:T(8,128)S(1)}, s32[1,4,128,256]{3,2,1,0:T(8,128)}, u32[]{:S(2)}) %copy-start.1) | copy-done | bytes 524312
  3.4 0.0 copy-start.2
  3.4 1.0 %copy-done.2 = f32[1,4,128,256]{3,2,1,0:T(8,128)S(1)} copy-done((f32[1,4,128,256]{3,2,1,0:T(8,128)S(1)}, f32[1,4,128,256]{3,2,1,0:T(8,128)}, u32[]{:S(2)}) %copy-start.2) | copy-done | bytes 524312
  4.4 0.0 copy-start.3
  4.4 1.0 %copy-done.3 = f32[4,128,256]{2,1,0:T(8,128)S(1)} copy-done((f32[4,128,256]{2,1,0:T(8,128)S(1)}, f32[4,128,256]{2,1,0:T(8,128)}, u32[]{:S(2)}) %copy-start.3) | copy-done | bytes 524312
  5.4 0.0 copy-start.4
  5.4 0.9 %copy-done.4 = f32[1,128,256]{2,1,0:T(8,128)S(1)} copy-done((f32[1,128,256]{2,1,0:T(8,128)S(1)}, f32[1,128,256]{2,1,0:T(8,128)}, u32[]{:S(2)}) %copy-start.4) | copy-done | bytes 131096
  6.4 22.5 %shard_map.77 = (f32[1,4,128,256]{3,2,1,0:T(8,128)S(1)}, f32[2,64,128]{2,1,0:T(8,128)S(1)}) custom-call(f32[1,4,128,256]{3,2,1,0:T(8,128)S(1)} %copy-done, s32[1,4,128,256]{3,2,1,0:T(8,128)S(1)} %copy-done.1, f32[1,4,128,256]{3,2,1,0:T(8,128)S(1)} %copy-done.2, f32[1,128,256]{2,1,0:T(8,128)S(1)} %copy-done.4, s32[1]{0:T(128)S(6)} %copy.10.cell_ref, ...), custom_call_target="tpu_custom_call" | custom-call | tf_op jit(solution)/shard_map/pallas_call | solution.py:368
  28.8 0.8 %copy.11 = f32[1,4,128,256]{3,2,1,0:T(8,128)} copy(f32[1,4,128,256]{3,2,1,0:T(8,128)S(1)} %get-tuple-element.4) | data formatting | bytes 1048576
  29.6 0.6 %copy.12 = f32[2,64,128]{2,1,0:T(8,128)} copy(f32[2,64,128]{2,1,0:T(8,128)S(1)} %get-tuple-element.5) | data formatting | bytes 131072
Async XLA Ops:
  1.3 1.0 %copy-start = (f32[1,4,128,256]{3,2,1,0:T(8,128)S(1)}, f32[1,4,128,256]{3,2,1,0:T(8,128)}, u32[]{:S(2)}) copy-start(f32[1,4,128,256]{3,2,1,0:T(8,128)} %t_hbm.1) | copy-start | bytes 1572868
  2.3 1.0 %copy-start.1 = (s32[1,4,128,256]{3,2,1,0:T(8,128)S(1)}, s32[1,4,128,256]{3,2,1,0:T(8,128)}, u32[]{:S(2)}) copy-start(s32[1,4,128,256]{3,2,1,0:T(8,128)} %c_hbm.1) | copy-start | bytes 1572868
  3.4 1.0 %copy-start.2 = (f32[1,4,128,256]{3,2,1,0:T(8,128)S(1)}, f32[1,4,128,256]{3,2,1,0:T(8,128)}, u32[]{:S(2)}) copy-start(f32[1,4,128,256]{3,2,1,0:T(8,128)} %a_hbm.1) | copy-start | bytes 1572868
  4.4 1.0 %copy-start.3 = (f32[4,128,256]{2,1,0:T(8,128)S(1)}, f32[4,128,256]{2,1,0:T(8,128)}, u32[]{:S(2)}) copy-start(f32[4,128,256]{2,1,0:T(8,128)} %slow_hbm.1) | copy-start | bytes 1572868
  5.4 0.9 %copy-start.4 = (f32[1,128,256]{2,1,0:T(8,128)S(1)}, f32[1,128,256]{2,1,0:T(8,128)}, u32[]{:S(2)}) copy-start(f32[1,128,256]{2,1,0:T(8,128)} %res_hbm.1) | copy-start | bytes 393220

commit v2 on v1

--- a/solution.py
+++ b/solution.py
@@ -14,12 +14,12 @@
 def kernel(
     n_src, n_gz,
     t_hbm, c_hbm, a_hbm, res_hbm, cell_ref, slow_hbm,
-    out_hbm, coarse_hbm,
+    out, coarse,
     t, code, lam, lam1, res, slow,
     wlx, whx, wly, why, wlz, whz, diag,
     num, dface, fac, g_out, t_in, g_in,
-    pool, pairs, part, rs_in, total,
-    load_sem, t_send, t_recv, g_send, g_recv, rs_send, rs_recv, ag_send, ag_recv, out_sem,
+    pool, pairs, part, pair_in, pair_sum, all_in,
+    load_sem, t_send, t_recv, g_send, g_recv, pair_send, pair_recv, all_send, all_recv,
 ):
     L, NY, NX = t.shape
     K = NY // CH
@@ -51,6 +51,48 @@
     for l in order[:2]:
         load(("c", l), c_hbm.at[0, l], code.at[l])
         load(("a", l), a_hbm.at[0, l], lam.at[l])
+
+    def rows(k):
+        return pl.ds(pl.multiple_of(k * CH, CH), CH)
+
+    def t_copy(s, k):
+        return pltpu.make_async_remote_copy(
+            src_ref=t_hbm.at[0, layer[s], rows(k)], dst_ref=t_in.at[1 - s, rows(k)],
+            send_sem=t_send.at[s, k], recv_sem=t_recv.at[1 - s, k],
+            device_id={"gz": target[s]}, device_id_type=MESH)
+
+    def t_arrival(s, k):
+        return pltpu.make_async_remote_copy(
+            src_ref=t_hbm.at[0, layer[s], rows(k)], dst_ref=t_in.at[s, rows(k)],
+            send_sem=t_send.at[s, k], recv_sem=t_recv.at[s, k],
+            device_id={"gz": target[s]}, device_id_type=MESH)
+
+    def g_copy(sweep, s, k):
+        return pltpu.make_async_remote_copy(
+            src_ref=g_out.at[sweep, s, rows(k)], dst_ref=g_in.at[sweep, 1 - s, rows(k)],
+            send_sem=g_send.at[sweep, s, k], recv_sem=g_recv.at[sweep, 1 - s, k],
+            device_id={"gz": target[s]}, device_id_type=MESH)
+
+    def g_arrival(sweep, s, k):
+        return pltpu.make_async_remote_copy(
+            src_ref=g_out.at[sweep, s, rows(k)], dst_ref=g_in.at[sweep, s, rows(k)],
+            send_sem=g_send.at[sweep, s, k], recv_sem=g_recv.at[sweep, s, k],
+            device_id={"gz": target[s]}, device_id_type=MESH)
+
+    pl.semaphore_wait(
+        barrier, n_src - 1 + has_lo.astype(jnp.int32) + has_hi.astype(jnp.int32)
+    )
+
+    def send_t(k):
+        for s in range(2):
+            @pl.when(exists[s])
+            def _(s=s):
+                t_copy(s, k).start()
+
+    AHEAD = 2
+    for k in range(min(AHEAD, K)):
+        send_t(k)
+
     for l in order:
         load(("t", l), t_hbm.at[0, l], t.at[l])
     for l in order[2:]:
@@ -60,33 +102,6 @@
     for l in range(L):
         load(("s", l), slow_hbm.at[l], slow.at[l])
 
-    def rows(k):
-        return pl.ds(pl.multiple_of(k * CH, CH), CH)
-
-    def t_copy(s, k):
-        return pltpu.make_async_remote_copy(
-            src_ref=t_hbm.at[0, layer[s], rows(k)], dst_ref=t_in.at[1 - s, rows(k)],
-            send_sem=t_send.at[s, k], recv_sem=t_recv.at[1 - s, k],
-            device_id={"gz": target[s]}, device_id_type=MESH)
-
-    def t_arrival(s, k):
-        return pltpu.make_async_remote_copy(
-            src_ref=t_hbm.at[0, layer[s], rows(k)], dst_ref=t_in.at[s, rows(k)],
-            send_sem=t_send.at[s, k], recv_sem=t_recv.at[s, k],
-            device_id={"gz": target[s]}, device_id_type=MESH)
-
-    def g_copy(sweep, s, k):
-        return pltpu.make_async_remote_copy(
-            src_ref=g_out.at[sweep, s, rows(k)], dst_ref=g_in.at[sweep, 1 - s, rows(k)],
-            send_sem=g_send.at[sweep, s, k], recv_sem=g_recv.at[sweep, 1 - s, k],
-            device_id={"gz": target[s]}, device_id_type=MESH)
-
-    def g_arrival(sweep, s, k):
-        return pltpu.make_async_remote_copy(
-            src_ref=g_out.at[sweep, s, rows(k)], dst_ref=g_in.at[sweep, s, rows(k)],
-            send_sem=g_send.at[sweep, s, k], recv_sem=g_recv.at[sweep, s, k],
-            device_id={"gz": target[s]}, device_id_type=MESH)
-
     for s in range(2):
         @pl.when(jnp.logical_not(exists[s]))
         def _(s=s):
@@ -98,10 +113,6 @@
         loads["c", l].wait()
         loads["a", l].wait()
 
-    pl.semaphore_wait(
-        barrier, n_src - 1 + has_lo.astype(jnp.int32) + has_hi.astype(jnp.int32)
-    )
-
     def factors(c, shift):
         factor = jnp.where((c & (4 << shift)) != 0, f32(2.0), f32(1.0))
         low = jnp.where((c & (1 << shift)) != 0, factor, f32(0.0))
@@ -110,16 +121,15 @@
 
     def first_sends(k, carry):
         for s in range(2):
-            @pl.when(exists[s])
-            def _(s=s):
-                t_copy(s, k).start()
-        for s in range(2):
             f = factors(code[layer[s], rows(k)], 6)[s]
             fac[s, rows(k)] = f
             g_out[0, s, rows(k)] = f * lam[layer[s], rows(k)]
             @pl.when(exists[s])
             def _(s=s):
                 g_copy(0, s, k).start()
+        @pl.when(k + AHEAD < K)
+        def _():
+            send_t(k + AHEAD)
         return carry
 
     lax.fori_loop(0, K, first_sends, 0)
@@ -247,34 +257,45 @@
     lax.fori_loop(0, K, first_faces, 0)
 
     def second_local(k, carry):
-        local_sweep(lam1, lam, k)
+        local_sweep(lam1, out.at[0], k)
         return carry
 
     lax.fori_loop(0, K, second_local, 0)
 
-    def out_copy(l):
-        return pltpu.make_async_copy(lam.at[l], out_hbm.at[0, l], out_sem.at[l])
-
-    for l in range(1, L - 1):
-        out_copy(l).start()
     for l in range(L):
         loads["s", l].wait()
 
     CR = CH // 2
-    CY = NY // 2
-    SR = (L // 2) * CY // n_src
-
-    def rs_copy(o):
-        return pltpu.make_async_remote_copy(
-            src_ref=part.at[pl.ds(pl.multiple_of(o * SR, SR), SR)], dst_ref=rs_in.at[me_s],
-            send_sem=rs_send.at[o], recv_sem=rs_recv.at[me_s],
-            device_id={"src": o}, device_id_type=MESH)
-
-    def rs_arrival(j):
-        return pltpu.make_async_remote_copy(
-            src_ref=part.at[pl.ds(0, SR)], dst_ref=rs_in.at[j],
-            send_sem=rs_send.at[j], recv_sem=rs_recv.at[j],
+    HALF = (L // 2) * CR // 2
+    partner = me_s + 1 - 2 * lax.rem(me_s, 2)
+    mine = lax.rem(me_s, 2)
+
+    def pair_copy(k):
+        return pltpu.make_async_remote_copy(
+            src_ref=part.at[k, 1 - mine], dst_ref=pair_in.at[k],
+            send_sem=pair_send.at[k], recv_sem=pair_recv.at[k],
+            device_id={"src": partner}, device_id_type=MESH)
+
+    def all_copy(k, i):
+        return pltpu.make_async_remote_copy(
+            src_ref=pair_sum.at[k], dst_ref=all_in.at[k, me_s],
+            send_sem=all_send.at[k, i], recv_sem=all_recv.at[k, me_s],
+            device_id={"src": lax.rem(me_s + i, n_src)}, device_id_type=MESH)
+
+    def all_arrival(k, i):
+        j = lax.rem(me_s + i, n_src)
+        return pltpu.make_async_remote_copy(
+            src_ref=pair_sum.at[k], dst_ref=all_in.at[k, j],
+            send_sem=all_send.at[k, i], recv_sem=all_recv.at[k, j],
             device_id={"src": j}, device_id_type=MESH)
+
+    def share(k):
+        pair_copy(k).wait_recv()
+        both = part[k, mine] + pair_in[k]
+        pair_sum[k] = both
+        for i in range(1, n_src):
+            all_copy(k, i).start()
+        all_in[k, me_s] = both
 
     def last_faces(k, carry):
         r = rows(k)
@@ -283,56 +304,24 @@
             @pl.when(exists[s])
             def _(s=s):
                 g_arrival(1, s, k).wait_recv()
-            lam[l, r] = (num[s, r] + dface[s, r] * g_in[1, s, r]) * diag[l, r]
+            out[0, l, r] = (num[s, r] + dface[s, r] * g_in[1, s, r]) * diag[l, r]
         for j in range(L // 2):
-            prod = lam[2 * j, r] * slow[2 * j, r] + lam[2 * j + 1, r] * slow[2 * j + 1, r]
+            prod = out[0, 2 * j, r] * slow[2 * j, r] + out[0, 2 * j + 1, r] * slow[2 * j + 1, r]
             hi = prod.astype(jnp.bfloat16)
             lo = (prod - hi.astype(f32)).astype(jnp.bfloat16)
             pairs[j] = jnp.dot(hi, pool[...], preferred_element_type=f32) + jnp.dot(
                 lo, pool[...], preferred_element_type=f32)
-            first = j * CY + k * CR
-            part[pl.ds(pl.multiple_of(first, CR), CR)] = (
-                pairs[j, pl.ds(0, CR, stride=2)] + pairs[j, pl.ds(1, CR, stride=2)])
-            for i in range(CR // SR):
-                o = first // SR + i
-                @pl.when(o != me_s)
-                def _(o=o):
-                    rs_copy(o).start()
+            sums = pairs[j, pl.ds(0, CR, stride=2)] + pairs[j, pl.ds(1, CR, stride=2)]
+            for h in range(2):
+                part[k, h, pl.ds(j * CR // 2, CR // 2)] = sums[h * CR // 2:(h + 1) * CR // 2]
+        pair_copy(k).start()
+        @pl.when(k > 0)
+        def _():
+            share(k - 1)
         return carry
 
     lax.fori_loop(0, K, last_faces, 0)
-    for s in range(2):
-        out_copy(layer[s]).start()
-
-    mine = pl.multiple_of(me_s * SR, SR)
-    acc = part[pl.ds(mine, SR)]
-    for i in range(1, n_src):
-        j = lax.rem(me_s + i, n_src)
-        rs_arrival(j).wait_recv()
-        acc = acc + rs_in[j]
-    total[...] = acc
-
-    def place(o):
-        return coarse_hbm.at[o * SR // CY, pl.ds(pl.multiple_of(lax.rem(o * SR, CY), SR), SR)]
-
-    def ag_copy(i):
-        o = lax.rem(me_s + i, n_src)
-        return pltpu.make_async_remote_copy(
-            src_ref=total, dst_ref=place(me_s),
-            send_sem=ag_send.at[i], recv_sem=ag_recv.at[i],
-            device_id={"src": o}, device_id_type=MESH)
-
-    def ag_arrival(i):
-        j = lax.rem(me_s + n_src - i, n_src)
-        return pltpu.make_async_remote_copy(
-            src_ref=total, dst_ref=place(j),
-            send_sem=ag_send.at[i], recv_sem=ag_recv.at[i],
-            device_id={"src": j}, device_id_type=MESH)
-
-    for i in range(1, n_src):
-        ag_copy(i).start()
-    own = pltpu.make_async_copy(total, place(me_s), ag_send.at[0])
-    own.start()
+    share(K - 1)
 
     def drain(k, carry):
         for s in range(2):
@@ -341,29 +330,35 @@
                 t_copy(s, k).wait_send()
                 g_copy(0, s, k).wait_send()
                 g_copy(1, s, k).wait_send()
-        return carry
-
+        pair_copy(k).wait_send()
+        for i in range(1, n_src):
+            all_copy(k, i).wait_send()
+        return carry
+
+    def gather(k, carry):
+        for i in range(1, n_src):
+            all_arrival(k, i).wait_recv()
+        for h in range(2):
+            acc = all_in[k, h]
+            for chip in range(1, n_src // 2):
+                acc = acc + all_in[k, 2 * chip + h]
+            for j in range(L // 2):
+                first = pl.multiple_of(k * CR + h * CR // 2, CR // 2)
+                coarse[j, pl.ds(first, CR // 2)] = acc[j * CR // 2:(j + 1) * CR // 2]
+        return carry
+
+    lax.fori_loop(0, K, gather, 0)
     lax.fori_loop(0, K, drain, 0)
-    for i in range(1, n_src):
-        rs_copy(lax.rem(me_s + i, n_src)).wait_send()
-    for l in range(L):
-        out_copy(l).wait()
-    own.wait()
-    for i in range(1, n_src):
-        ag_copy(i).wait_send()
-    for i in range(1, n_src):
-        ag_arrival(i).wait_recv()
 
 
 def shards(n_src, n_gz, travel_times, upwind_codes, adjoint_state, surface_residual, source_cell, slowness):
     _, L, NY, NX = travel_times.shape
     K = NY // CH
     f32 = jnp.float32
-    rows_total = (L // 2) * (NY // 2)
-    share = rows_total // n_src
+    half = (L // 2) * (CH // 2) // 2
     field = pltpu.VMEM((L, NY, NX), f32)
     faces = pltpu.VMEM((2, NY, NX), f32)
-    any_spec = pl.BlockSpec(memory_space=pl.ANY)
+    hbm_spec = pl.BlockSpec(memory_space=pltpu.HBM)
     dma = pltpu.SemaphoreType.DMA
     return pl.pallas_call(
         functools.partial(kernel, n_src, n_gz),
@@ -371,8 +366,8 @@
             jax.ShapeDtypeStruct(travel_times.shape, f32),
             jax.ShapeDtypeStruct((L // 2, NY // 2, NX // 2), f32),
         ),
-        in_specs=[any_spec] * 4 + [pl.BlockSpec(memory_space=pltpu.SMEM), any_spec],
-        out_specs=(any_spec, any_spec),
+        in_specs=[hbm_spec] * 4 + [pl.BlockSpec(memory_space=pltpu.SMEM), hbm_spec],
+        out_specs=(pl.BlockSpec(memory_space=pltpu.VMEM),) * 2,
         scratch_shapes=[
             field, pltpu.VMEM((L, NY, NX), jnp.int32), field, field,
             pltpu.VMEM((NY, NX), f32), field,
@@ -381,18 +376,18 @@
             pltpu.VMEM((2, 2, NY, NX), f32), faces, pltpu.VMEM((2, 2, NY, NX), f32),
             pltpu.VMEM((NX, NX // 2), jnp.bfloat16),
             pltpu.VMEM((L // 2, CH, NX // 2), f32),
-            pltpu.VMEM((rows_total, NX // 2), f32),
-            pltpu.VMEM((n_src, share, NX // 2), f32),
-            pltpu.VMEM((share, NX // 2), f32),
+            pltpu.VMEM((K, 2, half, NX // 2), f32),
+            pltpu.VMEM((K, half, NX // 2), f32),
+            pltpu.VMEM((K, half, NX // 2), f32),
+            pltpu.VMEM((K, n_src, half, NX // 2), f32),
             dma((4 * L + 1,)),
             dma((2, K)), dma((2, K)), dma((2, 2, K)), dma((2, 2, K)),
-            dma((n_src,)), dma((n_src,)), dma((n_src,)), dma((n_src,)),
-            dma((L,)),
+            dma((K,)), dma((K,)), dma((K, n_src)), dma((K, n_src)),
         ],
         compiler_params=pltpu.CompilerParams(
             collective_id=0, has_side_effects=True, vmem_limit_bytes=48 * 1024 * 1024
         ),
-    )(travel_times, upwind_codes, adjoint_state, surface_residual, source_cell, slowness)
+    )(*[pltpu.with_memory_space_constraint(v, pltpu.HBM) for v in (travel_times, upwind_codes, adjoint_state, surface_residual)], source_cell, pltpu.with_memory_space_constraint(slowness, pltpu.HBM))
 
 
 def solution(mesh):

time: 30.6 us -> 23.7 us (0.77)
  local copies, waits for them, and re-layouts: 6.49 us -> 1.42 us
  Pallas kernels: 22.5 us -> 20.9 us
    unnamed x12 -> x2, local copies, waits for them, and re-layouts: 6.49 us -> 1.42 us
    pallas_call x1, Pallas kernels: 22.5 us -> 20.9 us  [shards(): pl.pallas_call(functools.partial(kernel, n_src, n_gz), out_shape=(jax.Sha...]
where the time goes in v2:
time: 23.7 us; the launch traced here: 23.6 us
  Pallas kernels  20.9 us (88%)
  local copies, waits for them, and re-layouts  1.42 us (6%)
  between operations  1.29 us (5%)
    pallas_call x1, Pallas kernels, shards(): pl.pallas_call(functools.partial(kernel, n_src, n_gz), out_shape=(jax.Sha...  20.9 us
    unnamed x2, local copies, waits for them, and re-layouts  1.42 us

profile of v2, /device:TPU:0, one launch (start us, length us, event | category | flops | bytes accessed | tf_op | source)
XLA Modules:
  0.0 23.6 jit_solution(13370749540891546108)
XLA Ops:
  1.3 20.9 %shard_map.77 = (f32[1,4,128,256]{3,2,1,0:T(8,128)S(1)}, f32[2,64,128]{2,1,0:T(8,128)S(1)}) custom-call(f32[1,4,128,256]{3,2,1,0:T(8,128)} %t_hbm.1, s32[1,4,128,256]{3,2,1,0:T(8,128)} %c_hbm.1, f32[1,4,128,256]{3,2,1,0:T(8,128)} %a_hbm.1, f32[1,128,256]{2,1,0:T(8,128)} %res_hbm.1, s32[1]{0:T(128)S(6)} %copy.10.cell_ref, f32[4,128,256]{2,1,0:T(8,128)} %slow_hbm.1), custom_call_target="tpu_custom_call" | custom-call | tf_op jit(solution)/shard_map/pallas_call | solution.py:363
  22.1 0.8 %copy.11 = f32[1,4,128,256]{3,2,1,0:T(8,128)} copy(f32[1,4,128,256]{3,2,1,0:T(8,128)S(1)} %get-tuple-element.4) | data formatting | bytes 1048576
  22.9 0.6 %copy.12 = f32[2,64,128]{2,1,0:T(8,128)} copy(f32[2,64,128]{2,1,0:T(8,128)S(1)} %get-tuple-element.5) | data formatting | bytes 131072

commit v3 on v2

--- a/solution.py
+++ b/solution.py
@@ -58,25 +58,25 @@
     def t_copy(s, k):
         return pltpu.make_async_remote_copy(
             src_ref=t_hbm.at[0, layer[s], rows(k)], dst_ref=t_in.at[1 - s, rows(k)],
-            send_sem=t_send.at[s, k], recv_sem=t_recv.at[1 - s, k],
+            send_sem=t_send.at[s], recv_sem=t_recv.at[1 - s, k],
             device_id={"gz": target[s]}, device_id_type=MESH)
 
     def t_arrival(s, k):
         return pltpu.make_async_remote_copy(
             src_ref=t_hbm.at[0, layer[s], rows(k)], dst_ref=t_in.at[s, rows(k)],
-            send_sem=t_send.at[s, k], recv_sem=t_recv.at[s, k],
+            send_sem=t_send.at[s], recv_sem=t_recv.at[s, k],
             device_id={"gz": target[s]}, device_id_type=MESH)
 
     def g_copy(sweep, s, k):
         return pltpu.make_async_remote_copy(
             src_ref=g_out.at[sweep, s, rows(k)], dst_ref=g_in.at[sweep, 1 - s, rows(k)],
-            send_sem=g_send.at[sweep, s, k], recv_sem=g_recv.at[sweep, 1 - s, k],
+            send_sem=g_send.at[sweep, s], recv_sem=g_recv.at[sweep, 1 - s, k],
             device_id={"gz": target[s]}, device_id_type=MESH)
 
     def g_arrival(sweep, s, k):
         return pltpu.make_async_remote_copy(
             src_ref=g_out.at[sweep, s, rows(k)], dst_ref=g_in.at[sweep, s, rows(k)],
-            send_sem=g_send.at[sweep, s, k], recv_sem=g_recv.at[sweep, s, k],
+            send_sem=g_send.at[sweep, s], recv_sem=g_recv.at[sweep, s, k],
             device_id={"gz": target[s]}, device_id_type=MESH)
 
     pl.semaphore_wait(
@@ -279,15 +279,14 @@
     def all_copy(k, i):
         return pltpu.make_async_remote_copy(
             src_ref=pair_sum.at[k], dst_ref=all_in.at[k, me_s],
-            send_sem=all_send.at[k, i], recv_sem=all_recv.at[k, me_s],
+            send_sem=all_send.at[k], recv_sem=all_recv.at[k],
             device_id={"src": lax.rem(me_s + i, n_src)}, device_id_type=MESH)
 
-    def all_arrival(k, i):
-        j = lax.rem(me_s + i, n_src)
-        return pltpu.make_async_remote_copy(
-            src_ref=pair_sum.at[k], dst_ref=all_in.at[k, j],
-            send_sem=all_send.at[k, i], recv_sem=all_recv.at[k, j],
-            device_id={"src": j}, device_id_type=MESH)
+    def all_done(k):
+        others = all_in.at[k, pl.ds(0, n_src - 1)]
+        return pltpu.make_async_remote_copy(
+            src_ref=others, dst_ref=others, send_sem=all_send.at[k], recv_sem=all_recv.at[k],
+            device_id={"src": partner}, device_id_type=MESH)
 
     def share(k):
         pair_copy(k).wait_recv()
@@ -312,43 +311,46 @@
             pairs[j] = jnp.dot(hi, pool[...], preferred_element_type=f32) + jnp.dot(
                 lo, pool[...], preferred_element_type=f32)
             sums = pairs[j, pl.ds(0, CR, stride=2)] + pairs[j, pl.ds(1, CR, stride=2)]
-            for h in range(2):
-                part[k, h, pl.ds(j * CR // 2, CR // 2)] = sums[h * CR // 2:(h + 1) * CR // 2]
+            part[k, j // (L // 4), pl.ds(j % (L // 4) * CR, CR)] = sums
         pair_copy(k).start()
         @pl.when(k > 0)
         def _():
             share(k - 1)
         return carry
 
+    def drain_faces(sems, sent):
+        for s in range(2):
+            @pl.when(exists[s])
+            def _(s=s):
+                pltpu.make_async_remote_copy(
+                    src_ref=sent.at[s], dst_ref=sent.at[s], send_sem=sems.at[s],
+                    recv_sem=t_recv.at[s, 0], device_id={"gz": target[s]}, device_id_type=MESH,
+                ).wait_send()
+
+    drain_faces(t_send, g_out.at[0])
+    drain_faces(g_send.at[0], g_out.at[0])
     lax.fori_loop(0, K, last_faces, 0)
     share(K - 1)
 
     def drain(k, carry):
-        for s in range(2):
-            @pl.when(exists[s])
-            def _(s=s):
-                t_copy(s, k).wait_send()
-                g_copy(0, s, k).wait_send()
-                g_copy(1, s, k).wait_send()
         pair_copy(k).wait_send()
-        for i in range(1, n_src):
-            all_copy(k, i).wait_send()
+        all_done(k).wait_send()
         return carry
 
     def gather(k, carry):
-        for i in range(1, n_src):
-            all_arrival(k, i).wait_recv()
+        all_done(k).wait_recv()
         for h in range(2):
             acc = all_in[k, h]
             for chip in range(1, n_src // 2):
                 acc = acc + all_in[k, 2 * chip + h]
-            for j in range(L // 2):
-                first = pl.multiple_of(k * CR + h * CR // 2, CR // 2)
-                coarse[j, pl.ds(first, CR // 2)] = acc[j * CR // 2:(j + 1) * CR // 2]
+            for j in range(L // 4):
+                first = pl.multiple_of(k * CR, CR)
+                coarse[h * (L // 4) + j, pl.ds(first, CR)] = acc[j * CR:(j + 1) * CR]
         return carry
 
     lax.fori_loop(0, K, gather, 0)
     lax.fori_loop(0, K, drain, 0)
+    drain_faces(g_send.at[1], g_out.at[1])
 
 
 def shards(n_src, n_gz, travel_times, upwind_codes, adjoint_state, surface_residual, source_cell, slowness):
@@ -381,8 +383,8 @@
             pltpu.VMEM((K, half, NX // 2), f32),
             pltpu.VMEM((K, n_src, half, NX // 2), f32),
             dma((4 * L + 1,)),
-            dma((2, K)), dma((2, K)), dma((2, 2, K)), dma((2, 2, K)),
-            dma((K,)), dma((K,)), dma((K, n_src)), dma((K, n_src)),
+            dma((2,)), dma((2, K)), dma((2, 2)), dma((2, 2, K)),
+            dma((K,)), dma((K,)), dma((K,)), dma((K,)),
         ],
         compiler_params=pltpu.CompilerParams(
             collective_id=0, has_side_effects=True, vmem_limit_bytes=48 * 1024 * 1024

time: 23.7 us -> 23 us (0.970)
  Pallas kernels: 20.9 us -> 20.1 us
    pallas_call x1, Pallas kernels: 20.9 us -> 20.1 us  [shards(): pl.pallas_call(functools.partial(kernel, n_src, n_gz), out_shape=(jax.Sha...]
where the time goes in v3:
time: 23 us; the launch traced here: 22.9 us
  Pallas kernels  20.1 us (87%)
  local copies, waits for them, and re-layouts  1.42 us (6%)
  between operations  1.29 us (6%)
    pallas_call x1, Pallas kernels, shards(): pl.pallas_call(functools.partial(kernel, n_src, n_gz), out_shape=(jax.Sha...  20.1 us
    unnamed x2, local copies, waits for them, and re-layouts  1.42 us

profile of v3, /device:TPU:0, one launch (start us, length us, event | category | flops | bytes accessed | tf_op | source)
XLA Modules:
  0.0 22.9 jit_solution(12644810679207250741)
XLA Ops:
  1.3 20.1 %shard_map.77 = (f32[1,4,128,256]{3,2,1,0:T(8,128)S(1)}, f32[2,64,128]{2,1,0:T(8,128)S(1)}) custom-call(f32[1,4,128,256]{3,2,1,0:T(8,128)} %t_hbm.1, s32[1,4,128,256]{3,2,1,0:T(8,128)} %c_hbm.1, f32[1,4,128,256]{3,2,1,0:T(8,128)} %a_hbm.1, f32[1,128,256]{2,1,0:T(8,128)} %res_hbm.1, s32[1]{0:T(128)S(6)} %copy.10.cell_ref, f32[4,128,256]{2,1,0:T(8,128)} %slow_hbm.1), custom_call_target="tpu_custom_call" | custom-call | tf_op jit(solution)/shard_map/pallas_call | solution.py:365
  21.4 0.8 %copy.11 = f32[1,4,128,256]{3,2,1,0:T(8,128)} copy(f32[1,4,128,256]{3,2,1,0:T(8,128)S(1)} %get-tuple-element.4) | data formatting | bytes 1048576
  22.2 0.6 %copy.12 = f32[2,64,128]{2,1,0:T(8,128)} copy(f32[2,64,128]{2,1,0:T(8,128)S(1)} %get-tuple-element.5) | data formatting | bytes 131072
